TPU v7x, 32 devices: a whole 2x2x4 slice. The times are simulated.
32 devices in a mesh: grp: 2 (over y), rad: 8 (over z, x), orb: 2 (over core).
Axes of the slice: x: 2, y: 2, z: 4, core: 2. Of those that a mesh axis runs over, the one named last changes fastest.
Arguments:
- occupied: bfloat16 [32, 2, 16, 3470], P('orb', None, 'rad'), may hold values from -6 to 6
- continuum: bfloat16 [2, 32, 3470], P(None, ('grp', 'rad')), parts along dimension 1, may hold values from -6 to 6
- harmonics: bfloat16 [3470, 961], P('orb'), may hold values from -1.6953125 to 1.6953125
- angle_weight: float32 [3470], replicated, may hold values from 0.0018 to 0.0072
- radial_weight: float32 [16], P('rad'), may hold values from 0.005 to 0.04
- radius: float32 [16], P('rad'), may hold values from 1 to 4, as said below
- harmonic_order: int32 [961], replicated, may hold values from 0 to 960, each once
Outputs:
- exchange_field: float32 [2, 32, 3470], P(None, ('grp', 'rad'), 'orb'), parts along dimension 1
There are 2 independent parts, one for each index of `grp`. A program takes and returns all parts, laid end to end along the dimension named above; an argument that names none is the same for every part. Nothing has to cross between parts.
Inputs may be any that keep to these rules, and one draw needn't show every extreme that they name: `radius`: radii increase strictly with the radial index.
All inputs are finite; a program needn't handle non-finite values.
Results may differ from a plain program's by a relative error of at most 0.0032.
Values may be sent and summed in bfloat16 or wider, within the bound.
A program may use at most 128 MiB of HBM per device.

v0:
```python
import jax
import jax.numpy as jnp
from jax import lax
from jax.sharding import PartitionSpec as P

LMAX = 30


FOUR_PI = 12.566370614359172


def carried_in(value, axis, join, neutral, backward):
    count, mine = (lax.axis_size(axis), lax.axis_index(axis))
    pieces = jax.tree.map(lambda part: lax.all_gather(part, axis), value)
    if backward:
        pieces = jax.tree.map(lambda part: part[::-1], pieces)
        mine = count - 1 - mine
    running = jax.tree.map(
        lambda part, zero: jnp.full_like(part, 0) + jnp.asarray(zero, part.dtype), value, neutral
    )

    def step(position, running):
        longer = join(running, jax.tree.map(lambda part: part[position], pieces))
        return jax.tree.map(lambda new, old: jnp.where(position < mine, new, old), longer, running)

    return lax.fori_loop(0, count - 1, step, running)


def degree_of(harmonic_order):
    squares = (jnp.arange(1, LMAX + 1) ** 2).astype(jnp.int32)
    hits = (harmonic_order[:, None] >= squares[None, :]).astype(jnp.int32)
    return jnp.sum(hits, axis=1)


def pair_density(occupied, continuum, angle_weight):
    occ_real = occupied[:, 0].astype(jnp.float32)
    occ_imag = occupied[:, 1].astype(jnp.float32)
    cont_real = continuum[0].astype(jnp.float32)[None]
    cont_imag = continuum[1].astype(jnp.float32)[None]
    real_part = (occ_real * cont_real + occ_imag * cont_imag) * angle_weight
    imag_part = (occ_real * cont_imag - occ_imag * cont_real) * angle_weight
    return jnp.stack([real_part, imag_part], axis=1).astype(jnp.bfloat16)


def combine_field(occupied, grid_values):
    occ_real = occupied[:, 0].astype(jnp.float32)
    occ_imag = occupied[:, 1].astype(jnp.float32)
    real_part = jnp.sum(occ_real * grid_values[:, 0] - occ_imag * grid_values[:, 1], axis=0)
    imag_part = jnp.sum(occ_real * grid_values[:, 1] + occ_imag * grid_values[:, 0], axis=0)
    return jnp.stack([real_part, imag_part], axis=0)


def radial_potential(moments, radius, radial_weight, degree):
    charge = moments * radial_weight[None, None, :, None]
    row_count = radius.shape[0]
    position = jnp.arange(row_count)
    lower_mask = position[None, :] <= position[:, None]
    upper_mask = position[None, :] > position[:, None]
    ratio_low = jnp.where(lower_mask, radius[None, :] / radius[:, None], 1.0)
    ratio_high = jnp.where(upper_mask, radius[:, None] / radius[None, :], 1.0)
    inner_kernel = jnp.where(
        lower_mask[:, :, None], jnp.power(ratio_low[:, :, None], degree[None, None, :]), 0.0
    )
    outer_kernel = jnp.where(
        upper_mask[:, :, None], jnp.power(ratio_high[:, :, None], degree[None, None, :]), 0.0
    )
    scaled = charge / radius[None, None, :, None]
    inner_local = jnp.einsum(
        "kjm,ocjm->ockm", inner_kernel, charge, precision=lax.Precision.HIGHEST
    )
    outer_local = jnp.einsum(
        "kjm,ocjm->ockm", outer_kernel, scaled, precision=lax.Precision.HIGHEST
    )
    zero_anchor = jnp.zeros((), radius.dtype)
    empty_sum = jnp.zeros_like(charge[:, :, 0, :])

    def join_inner(earlier, later_part):
        total_a, edge_a = earlier
        total_b, edge_b = later_part
        is_live = edge_b > 0
        ratio_join = jnp.where(is_live, edge_a / jnp.where(is_live, edge_b, 1.0), 1.0)
        joined = jnp.power(ratio_join, degree) * total_a + total_b
        return (jnp.where(is_live, joined, total_a), jnp.where(is_live, edge_b, edge_a))

    def join_outer(earlier, later_part):
        total_a, edge_a = earlier
        total_b, edge_b = later_part
        is_live = edge_b > 0
        ratio_join = jnp.where(edge_a > 0, edge_b / jnp.where(edge_a > 0, edge_a, 1.0), 0.0)
        joined = total_b + jnp.power(ratio_join, degree) * total_a
        return (jnp.where(is_live, joined, total_a), jnp.where(is_live, edge_b, edge_a))

    inner_in, edge_in = carried_in(
        (inner_local[:, :, row_count - 1, :], radius[row_count - 1]),
        "rad",
        join_inner,
        (empty_sum, zero_anchor),
        False,
    )
    outer_in, edge_out = carried_in(
        (scaled[:, :, 0, :] + outer_local[:, :, 0, :], radius[0]),
        "rad",
        join_outer,
        (empty_sum, zero_anchor),
        True,
    )
    lift_inner = jnp.power((edge_in / radius)[:, None], degree[None, :])
    reach_ratio = jnp.where(edge_out > 0, radius / jnp.where(edge_out > 0, edge_out, 1.0), 0.0)
    lift_outer = jnp.power(reach_ratio[:, None], degree[None, :])
    inner_sum = inner_local + lift_inner[None, None] * inner_in[:, :, None, :]
    outer_sum = outer_local + lift_outer[None, None] * outer_in[:, :, None, :]
    factor = FOUR_PI / (2.0 * degree + 1.0)
    return (factor * (inner_sum / radius[None, None, :, None] + outer_sum)).astype(jnp.bfloat16)


def on_device(occupied, continuum, harmonics, angle_weight, radial_weight, radius, harmonic_order):
    degree = degree_of(harmonic_order).astype(jnp.float32)
    orbitals = occupied.shape[0]
    radial = occupied.shape[2]
    modes = harmonics.shape[1]
    density = pair_density(occupied, continuum, angle_weight)
    flat_density = density.reshape(orbitals * 2 * radial, density.shape[3])
    moments = jnp.dot(
        flat_density,
        lax.all_gather(harmonics, "orb", axis=0, tiled=True),
        preferred_element_type=jnp.float32,
    )
    potential = radial_potential(
        moments.reshape(orbitals, 2, radial, modes), radius, radial_weight, degree
    )
    flat_potential = potential.reshape(orbitals * 2 * radial, modes)
    table_piece = lax.all_gather(harmonics, "orb", axis=0, tiled=True)
    span_width = table_piece.shape[0]
    grid_values = lax.dot_general(
        flat_potential, table_piece, (((1,), (1,)), ((), ())), preferred_element_type=jnp.float32
    )
    grid_values = grid_values.reshape(orbitals, 2, radial, span_width)
    partial_field = combine_field(occupied, grid_values)
    return lax.psum_scatter(partial_field, "orb", scatter_dimension=2, tiled=True)


def solution(mesh):
    placed = (
        P("orb", None, "rad", None),
        P(None, ("grp", "rad"), None),
        P("orb", None),
        P(),
        P("rad"),
        P("rad"),
        P(),
    )
    return jax.shard_map(
        on_device,
        mesh=mesh,
        in_specs=placed,
        out_specs=P(None, ("grp", "rad"), "orb"),
        check_vma=False,
    )
```

profile of v0, /device:TPU:0, one launch (start us, length us, event | category | flops | bytes accessed | tf_op | source)
XLA Modules:
  0.0 245.0 jit_solution(14857719136286107006)
XLA Ops:
  6.6 0.7 all-gather.5.cloned.1.call-update
  7.9 0.7 slice_dynamic-update-slice_fusion
  8.6 0.8 slice_dynamic-update-slice_fusion.1
  9.5 23.1 %all-reduce.3 = (f32[8]{0:T(128)S(1)}, f32[8]{0:T(128)S(1)}) all-reduce(f32[8]{0:T(128)S(1)} %slice_dynamic-update-slice_fusion, f32[8]{0:T(128)S(1)} %slice_dynamic-update-slice_fusion.1), channel_id=1, replica_groups=mesh['grp'=2,'rad'=8,'orb'=2] {'rad'}, use_global_device_ids=true, to_apply=%add.1 | all-reduce | flops 16 | bytes 128
  32.8 0.6 dynamic-slice.2
  34.7 28.6 %copy.32 = bf16[2,1735,961]{1,0,2:T(2,128)(2,1)} copy(bf16[2,1735,961]{1,2,0:T(8,128)(2,1)} %all-gather.5.cloned.1.call-done) | data formatting | bytes 13338680 | tf_op jit(solution)/shard_map/all_gather | solution.py:125
  63.3 15.5 %reshape.229 = bf16[3470,961,1,1]{0,1,2,3:T(8,128)(2,1)} reshape(bf16[2,1735,961]{1,0,2:T(2,128)(2,1)} %copy.32) | data formatting | bytes 13338680
  78.8 5.9 %broadcast_divide_fusion = (f32[16,2,2,961]{3,0,2,1:T(8,128)S(1)}, f32[16,2,2,961]{3,0,2,1:T(8,128)}) fusion(f32[2]{0:T(128)S(1)} %copy-done.3, f32[2]{0:T(128)S(1)} %copy-done.6, bf16[3470,961,1,1]{0,1,2,3:T(8,128)(2,1)} %reshape.229, bf16[16,1,2,3470]{3,0,2,1:T(8,128)(2,1)S(1)} %get-tuple-element.361, bf16[16,1,2,3470]{3,0,2,1:T(8,128)(2,1)S(1)} %get-tuple-element.360), kind=kOutput, calls=%fused_computation.54 | convolution fusion | flops 427182848 | bytes 7605548 | tf_op jit(solution)/shard_map/dot_general | solution.py:123
  84.7 2.2 copy.37
  86.9 15.1 %fusion.8 = f32[961,16,2,2]{1,3,2,0:T(2,128)S(1)} fusion(f32[16,2,2,961]{0,2,1,3:T(2,128)} %copy.37, pred[2,2]{1,0:T(4,128)(4,1)S(1)} %iota_compare_fusion, f32[2,2]{1,0:T(2,128)S(1)} %get-tuple-element.371, f32[961]{0:T(1024)S(1)} %convert_element_type.44), kind=kOutput, calls=%fused_computation.13 | convolution fusion | flops 1479940 | bytes 495896 | tf_op jit(solution)/shard_map/kjm,ocjm->ockm/dot_general | solution.py:71
  101.9 1.6 copy.38
  103.6 33.8 %all-gather.1 = f32[128,2,1,961]{3,0,2,1:T(8,128)S(1)} all-gather(f32[16,2,1,961]{3,0,2,1:T(8,128)S(1)} %slice_add_fusion), channel_id=3, replica_groups=mesh['grp'=2,'rad'=8,'orb'=2] {'rad'}, dimensions={0}, use_global_device_ids=true | all-gather | bytes 1107072 | tf_op jit(solution)/shard_map/all_gather | solution.py:14
  137.3 0.8 copy.39
  138.2 18.9 %while.33 = (s32[]{:T(128)}, f32[16,2,961]{2,1,0:T(2,128)S(1)}, f32[]{:T(128)}, s32[]{:T(128)}, f32[8]{0:T(128)S(1)}, /*index=5*/f32[8,16,2,961]{3,2,1,0:T(2,128...) while((s32[]{:T(128)}, f32[16,2,961]{2,1,0:T(2,128)S(1)}, ...), condition=%wide.region_4.5_spmd.clone, body=%wide.region_3.4_spmd.clone.sunk | while | flops 153771 | bytes 380796 | solution.py:26
  138.5 0.6 dynamic_slice.41
  141.1 0.6 dynamic_slice.41
  143.8 0.6 dynamic_slice.41
  146.5 0.6 dynamic_slice.41
  149.1 0.6 dynamic_slice.41
  151.8 0.6 dynamic_slice.41
  154.5 0.6 dynamic_slice.41
  157.2 1.8 copy.33
  159.0 15.0 %fusion.10 = f32[961,16,2,2]{1,3,2,0:T(2,128)} fusion(f32[16,2,2,961]{0,2,1,3:T(2,128)S(1)} %copy.33, pred[2,2]{1,0:T(4,128)(4,1)S(1)} %iota_compare_fusion.1, f32[2,2]{1,0:T(2,128)S(1)} %get-tuple-element.370, f32[961]{0:T(1024)S(1)} %get-tuple-element.530), kind=kOutput, calls=%fused_computation.15 | convolution fusion | flops 1479940 | bytes 495896 | tf_op jit(solution)/shard_map/kjm,ocjm->ockm/dot_general | solution.py:68
  173.9 2.6 %copy.34 = f32[961,16,2,2]{0,1,3,2:T(8,128)S(1)} copy(f32[961,16,2,2]{1,3,2,0:T(2,128)} %fusion.10) | data formatting | bytes 492032 | tf_op jit(solution)/shard_map/kjm,ocjm->ockm/dot_general | solution.py:68
  176.6 32.4 %all-gather = f32[128,2,1,961]{3,0,2,1:T(8,128)S(1)} all-gather(f32[16,2,1,961]{3,0,2,1:T(8,128)S(1)} %slice.48), channel_id=2, replica_groups=mesh['grp'=2,'rad'=8,'orb'=2] {'rad'}, dimensions={0}, use_global_device_ids=true | all-gather | bytes 1107072 | tf_op jit(solution)/shard_map/all_gather | solution.py:14
  208.9 20.0 %while.32 = (s32[]{:T(128)}, f32[16,2,961]{2,1,0:T(2,128)S(1)}, f32[]{:T(128)}, s32[]{:T(128)}, f32[8]{0:T(128)S(1)}, /*index=5*/f32[961]{0:T(1024)S(1)}, f32[8,...) while((s32[]{:T(128)}, f32[16,2,961]{2,1,0:T(2,128)S(1)}, ...), condition=%wide.region_2.3_spmd.clone, body=%wide.region_1.2_spmd.clone.sunk | while | flops 153770 | bytes 626803 | solution.py:26
  209.0 0.6 dynamic_slice.39
  211.8 0.6 dynamic_slice.39
  214.7 0.6 dynamic_slice.39
  229.2 4.4 %fusion.1 = f32[16,2,2,3470]{3,0,2,1:T(8,128)S(1)} fusion(bf16[3470,961,1,1]{0,1,2,3:T(8,128)(2,1)} %reshape.229, f32[16,2,961]{2,0,1:T(8,128)S(1)} %copy.40, f32[2,961]{1,0:T(2,128)S(1)} %get-tuple-element.367, f32[2]{0:T(128)S(1)} %copy-done.3, f32[16,2,961]{2,0,1:T(8,128)S(1)} %copy.36, f32[2,961]{1,0:T(2,128)S(1)} %get-tuple-element.366, ...), kind=kOutput, calls=%fused_computation.8 | convolution fusion | flops 427329792 | bytes 8314936 | tf_op jit(solution)/shard_map/dot_general | solution.py:134
  233.9 3.6 %all-reduce.2 = f32[2,2,3470]{2,1,0:T(2,128)S(1)} all-reduce(f32[2,2,3470]{2,1,0:T(2,128)S(1)} %pad_maximum_fusion), channel_id=4, replica_groups=mesh['grp'=2,'rad'=8,'orb'=2] {'orb'}, use_global_device_ids=true, to_apply=%region_7.8.clone | all-reduce | flops 13880 | bytes 111040
  237.5 0.7 constant_dynamic-slice_fusion.1
  (84 shorter events, 7.2 us)
Async XLA Ops:
  6.5 0.8 copy-start.8
  6.5 26.2 %copy-start.7 = (u32[32]{0:T(128)S(1)}, u32[32]{0:T(128)}, u32[]{:S(2)}) copy-start(u32[32]{0:T(128)} %constant.109) | copy-start | bytes 388
  6.5 1.4 copy-start.3
  6.5 26.1 %copy-start.5 = (s32[961]{0:T(1024)S(1)}, s32[961]{0:T(1024)}, u32[]{:S(2)}) copy-start(s32[961]{0:T(1024)} %param.17) | copy-start | bytes 11536
  6.5 27.6 %copy-start.2 = (bf16[2,2,3470]{2,1,0:T(2,128)(2,1)S(1)}, bf16[2,2,3470]{2,1,0:T(2,128)(2,1)}, u32[]{:S(2)}) copy-start(bf16[2,2,3470]{2,1,0:T(2,128)(2,1)} %param.12) | copy-start | bytes 83284
  6.5 27.6 %copy-start.1 = (bf16[16,2,2,3470]{3,2,1,0:T(2,128)(2,1)S(1)}, bf16[16,2,2,3470]{3,2,1,0:T(2,128)(2,1)}, u32[]{:S(2)}) copy-start(bf16[16,2,2,3470]{3,2,1,0:T(2,128)(2,1)} %param.11) | copy-start | bytes 1332484
  6.6 28.1 %all-gather.5.cloned.1.call-start = ((), (), s32[]{:S(2)}) async-start(), calls=%async_computation | async-start | bytes 10407936 | tf_op jit(solution)/shard_map/all_gather | solution.py:125
  6.6 27.9 %copy-start.4 = (f32[3470]{0:T(1024)S(1)}, f32[3470]{0:T(1024)}, u32[]{:S(2)}) copy-start(f32[3470]{0:T(1024)} %param.14) | copy-start | bytes 41644
  63.3 15.5 %copy-start.6 = (f32[2]{0:T(128)S(1)}, f32[2]{0:T(128)}, u32[]{:S(2)}) copy-start(f32[2]{0:T(128)} %param.15) | copy-start | bytes 28
  138.1 19.0 %copy-start = (f32[16,2,2,961]{3,0,2,1:T(8,128)S(1)}, f32[16,2,2,961]{3,0,2,1:T(8,128)}, u32[]{:S(2)}) copy-start(f32[16,2,2,961]{3,0,2,1:T(8,128)} %get-tuple-element.373) | copy-start | bytes 738052
Sparse Core Ops, SparseCore 0:
  8.9 20.4 all-gather.4
where the time goes:
time: 246 us; the launch traced here: 245 us
  blocking collectives  92.8 us (38%)
  local copies, waits for them, and re-layouts  66.1 us (27%)
  matrix products  40.3 us (16%)
  loops' own time  27.7 us (11%)
  between operations  14.3 us (6%)
  other arithmetic  3.1 us (1%)
    all_gather x2, blocking collectives, carried_in(): pieces = jax.tree.map(lambda part: lax.all_gather(part, axis), value)  66.2 us
    all_gather x1, local copies, waits for them, and re-layouts, on_device(): lax.all_gather(harmonics, 'orb', axis=0, tiled=True)  28.6 us
    another operation x2, loops' own time, carried_in(): return lax.fori_loop(0, count - 1, step, running)  27.7 us
    unnamed x2, blocking collectives  26.7 us
    unnamed x26, local copies, waits for them, and re-layouts  19 us
    dot_general x1, matrix products, radial_potential(): jnp.einsum('kjm,ocjm->ockm', outer_kernel, scaled, precision=lax.Precisio...  15.1 us
    dot_general x1, matrix products, radial_potential(): jnp.einsum('kjm,ocjm->ockm', inner_kernel, charge, precision=lax.Precisio...  15 us
    dynamic_slice x21, local copies, waits for them, and re-layouts, step(): longer = join(running, jax.tree.map(lambda part: part[position], pieces))  8.53 us
  transfers between devices with their start and end apart: 1, of which 0 were waited for; matrix products, arithmetic and copies ran while one was open for 1% of the time, Pallas kernels for 0%

commit v1 on v0

v1 whole, which is shorter than its diff:
```python
import functools

import jax
import jax.numpy as jnp
from jax import lax
from jax.experimental import pallas as pl
from jax.experimental.pallas import tpu as pltpu
from jax.sharding import PartitionSpec as P

LMAX = 30
FOUR_PI = 12.566370614359172
MESH = pl.DeviceIdType.MESH
LANES = 128
CHUNK = 256
F32 = jnp.float32
BF16 = jnp.bfloat16


def degree_of(harmonic_order):
    squares = (jnp.arange(1, LMAX + 1) ** 2).astype(jnp.int32)
    hits = (harmonic_order[:, None] >= squares[None, :]).astype(jnp.int32)
    return jnp.sum(hits, axis=1)


def kernel(
    n_rad, io, points, modes,
    occ_ref, cont_ref, degree_ref, radius_ref, weight_ref, table_hbm, out_ref,
    table, occ_in, occ, cont, dens, m_own, m_send, m_recv, st, inbox, carried, carry, pot,
    table_sem, sib_send, sib_recv, m_send_sem, m_recv_sem, up_send, up_recv, back_send, back_recv,
):
    me, core = lax.axis_index("rad"), lax.axis_index("orb")
    sibling = 1 - core
    rows = 4 * io
    half = 2 * io
    units = st.shape[0]
    stride = n_rad // units
    wide = occ.shape[2]
    window = occ_in.shape[1]
    base = points // LANES * LANES
    shift = points - base
    chunks = m_own.shape[0]

    fetch = pltpu.make_async_copy(table_hbm, table, table_sem)
    fetch.start()

    barrier = pltpu.get_barrier_semaphore()
    pl.semaphore_signal(barrier, inc=1, device_id={"orb": sibling}, device_id_type=MESH)

    def greet(step, carry_in):
        other = lax.rem(me + step, n_rad)
        pl.semaphore_signal(barrier, inc=1, device_id={"rad": other}, device_id_type=MESH)
        return carry_in

    lax.fori_loop(1, n_rad, greet, 0)
    pl.semaphore_wait(barrier, n_rad)

    send_occ = pltpu.make_async_remote_copy(
        src_ref=occ_ref.at[:, pl.ds(pl.multiple_of(sibling * base, LANES), window)],
        dst_ref=occ_in,
        send_sem=sib_send.at[0],
        recv_sem=sib_recv.at[0],
        device_id={"orb": sibling},
        device_id_type=MESH,
    )
    send_occ.start()

    degree = degree_ref[...]
    r0, r1, w0, w1 = radius_ref[0], radius_ref[1], weight_ref[0], weight_ref[1]
    log0 = jnp.log(jnp.full(degree.shape, r0, F32))
    log1 = jnp.log(jnp.full(degree.shape, r1, F32))
    up0, up1 = jnp.exp(degree * log0), jnp.exp(degree * log1)
    down0, down1 = jnp.exp(-degree * log0), jnp.exp(-degree * log1)
    a0, a1 = up0 * w0, up1 * w1
    b0, b1 = jnp.exp(-(degree + 1.0) * log0) * w0, jnp.exp(-(degree + 1.0) * log1) * w1
    factor = FOUR_PI / (2.0 * degree + 1.0)

    mine = pl.ds(pl.multiple_of(core * base, LANES), window)

    def align(value):
        return pltpu.roll(value, lax.rem(window - core * shift, window), 1)[:, :wide]

    def make_density(slot):
        for k in range(2):
            real = occ[slot, k * half : k * half + io]
            imag = occ[slot, k * half + io : (k + 1) * half]
            c_real, c_imag = cont[2 * k : 2 * k + 1], cont[2 * k + 1 : 2 * k + 2]
            top = slot * rows + k * half
            dens[top : top + io] = (real * c_real + imag * c_imag).astype(BF16)
            dens[top + io : top + half] = (real * c_imag - imag * c_real).astype(BF16)

    cont[...] = align(cont_ref[:, mine])
    occ[0] = align(occ_ref[:, mine].astype(F32))
    make_density(0)
    m_send[chunks - 1] = jnp.zeros(m_send.shape[1:], F32)
    m_own[chunks - 1] = jnp.zeros(m_own.shape[1:], F32)

    send_occ.wait()
    occ[1] = align(occ_in[...].astype(F32))
    make_density(1)
    fetch.wait()

    def m_copy(c):
        return pltpu.make_async_remote_copy(
            src_ref=m_send.at[c],
            dst_ref=m_recv.at[c],
            send_sem=m_send_sem.at[c],
            recv_sem=m_recv_sem.at[c],
            device_id={"orb": sibling},
            device_id_type=MESH,
        )

    def project(c):
        count = min(CHUNK, modes - c * CHUNK)
        part = lax.dot_general(
            dens[:, :points],
            table[c * CHUNK : c * CHUNK + count, :],
            (((1,), (1,)), ((), ())),
            preferred_element_type=F32,
        )
        m_own[c, :, :count] = part[:rows]
        m_send[c, :, :count] = part[rows:]
        m_copy(c).start()

    def up_copy(u):
        return pltpu.make_async_remote_copy(
            src_ref=st.at[u],
            dst_ref=inbox.at[me],
            send_sem=up_send.at[u],
            recv_sem=up_recv.at[me],
            device_id={"rad": u * stride},
            device_id_type=MESH,
        )

    def summarise(c):
        m_copy(c).wait()
        total = m_own[c] + m_recv[c]
        m_own[c] = total
        for u in range(c * CHUNK // LANES, (c + 1) * CHUNK // LANES):
            cols = slice(u * LANES, (u + 1) * LANES)
            here = (u * LANES) % CHUNK
            m0 = total[:half, here : here + LANES]
            m1 = total[half:, here : here + LANES]
            st[u, :half] = (a0[:, cols] * m0 + a1[:, cols] * m1).astype(BF16)
            st[u, half:] = (b0[:, cols] * m0 + b1[:, cols] * m1).astype(BF16)

            @pl.when(me != u * stride)
            def _():
                up_copy(u).start()

    project(0)
    for c in range(1, chunks):
        project(c)
        summarise(c - 1)
    summarise(chunks - 1)

    my_unit = me // stride

    def back_copy(r):
        return pltpu.make_async_remote_copy(
            src_ref=carried.at[r],
            dst_ref=carry.at[my_unit],
            send_sem=back_send.at[r],
            recv_sem=back_recv.at[my_unit],
            device_id={"rad": r},
            device_id_type=MESH,
        )

    def own_unit():
        inbox[me] = st[my_unit]

        def receive(r, held):
            @pl.when(r != me)
            def _():
                pltpu.make_async_remote_copy(
                    src_ref=st.at[0],
                    dst_ref=inbox.at[r],
                    send_sem=up_send.at[0],
                    recv_sem=up_recv.at[r],
                    device_id={"rad": r},
                    device_id_type=MESH,
                ).wait_recv()
            return held

        def rising(r, total):
            carried[r, :half] = total.astype(BF16)
            return total + inbox[r, :half].astype(F32)

        def falling(step, total):
            r = n_rad - 1 - step
            carried[r, half:] = total.astype(BF16)

            @pl.when(r != me)
            def _():
                back_copy(r).start()

            return total + inbox[r, half:].astype(F32)

        zero = jnp.zeros((half, LANES), F32)
        lax.fori_loop(0, n_rad, receive, 0)
        lax.fori_loop(0, n_rad, rising, zero, unroll=n_rad <= 8)
        lax.fori_loop(0, n_rad, falling, zero, unroll=n_rad <= 8)
        carry[my_unit] = carried[me]

    if stride == 1:
        own_unit()
    else:
        pl.when(lax.rem(me, stride) == 0)(own_unit)

    for u in range(units):
        @pl.when(me != u * stride)
        def _():
            pltpu.make_async_remote_copy(
                src_ref=carried.at[0],
                dst_ref=carry.at[u],
                send_sem=back_send.at[0],
                recv_sem=back_recv.at[u],
                device_id={"rad": u * stride},
                device_id_type=MESH,
            ).wait_recv()

        cols = slice(u * LANES, (u + 1) * LANES)
        here = (u * LANES) % CHUNK
        total = m_own[u * LANES // CHUNK]
        m0 = total[:half, here : here + LANES]
        m1 = total[half:, here : here + LANES]
        inner = carry[u, :half].astype(F32)
        outer = carry[u, half:].astype(F32)
        inner0 = w0 * m0 + down0[:, cols] * inner
        outer0 = up0[:, cols] * (b1[:, cols] * m1 + outer)
        inner1 = w1 * m1 + down1[:, cols] * (a0[:, cols] * m0 + inner)
        outer1 = up1[:, cols] * outer
        pot[:half, cols] = (factor[:, cols] * (inner0 / r0 + outer0)).astype(BF16)
        pot[half:rows, cols] = (factor[:, cols] * (inner1 / r1 + outer1)).astype(BF16)

    send_pot = pltpu.make_async_remote_copy(
        src_ref=pot.at[0:rows],
        dst_ref=pot.at[rows : 2 * rows],
        send_sem=sib_send.at[1],
        recv_sem=sib_recv.at[1],
        device_id={"orb": sibling},
        device_id_type=MESH,
    )
    send_pot.start()
    send_pot.wait()

    potential = pot[:, :modes]
    for start in range(0, points, CHUNK):
        count = min(CHUNK, points - start)
        span = slice(start, start + count)
        grid = jnp.dot(potential, table[:, span], preferred_element_type=F32)
        for k in range(2):
            real_sum = imag_sum = None
            for slot in range(2):
                top = k * half
                o_real = occ[slot, top : top + io, span]
                o_imag = occ[slot, top + io : top + half, span]
                top += slot * rows
                g_real, g_imag = grid[top : top + io], grid[top + io : top + half]
                real = o_real * g_real - o_imag * g_imag
                imag = o_real * g_imag + o_imag * g_real
                real_sum = real if slot == 0 else real_sum + real
                imag_sum = imag if slot == 0 else imag_sum + imag
            out_ref[k : k + 1, span] = jnp.sum(real_sum, axis=0, keepdims=True)
            out_ref[2 + k : 3 + k, span] = jnp.sum(imag_sum, axis=0, keepdims=True)

    for u in range(units):
        @pl.when(me != u * stride)
        def _():
            up_copy(u).wait_send()

    def finish():
        def sent(r, held):
            @pl.when(r != me)
            def _():
                back_copy(r).wait_send()
            return held

        lax.fori_loop(0, n_rad, sent, 0)

    if stride == 1:
        finish()
    else:
        pl.when(lax.rem(me, stride) == 0)(finish)


def on_device(occupied, continuum, harmonics, angle_weight, radial_weight, radius, harmonic_order):
    io, _, radial, total_points = occupied.shape
    points, modes = harmonics.shape
    n_rad = lax.axis_size("rad")
    padded = -(-modes // CHUNK) * CHUNK
    units, chunks = padded // LANES, padded // CHUNK
    base = points // LANES * LANES
    wide = -(-points // LANES) * LANES
    window = -(-total_points // LANES) * LANES - base
    lanes_in = base + window
    rows = 4 * io
    half = 2 * io

    fill = ((0, 0), (0, lanes_in - total_points))
    occ_rows = jnp.pad(jnp.transpose(occupied, (2, 1, 0, 3)).reshape(rows, total_points), fill)
    weighted = continuum.astype(F32) * angle_weight
    cont_rows = jnp.pad(jnp.transpose(weighted, (1, 0, 2)).reshape(4, total_points), fill)
    degree = jnp.pad(degree_of(harmonic_order).astype(F32), (0, padded - modes))[None]

    vmem = pl.BlockSpec(memory_space=pltpu.VMEM)
    smem = pl.BlockSpec(memory_space=pltpu.SMEM)
    dma = pltpu.SemaphoreType.DMA
    field = pl.pallas_call(
        functools.partial(kernel, n_rad, io, points, modes),
        out_shape=jax.ShapeDtypeStruct((4, points), F32),
        in_specs=[vmem, vmem, vmem, smem, smem, pl.BlockSpec(memory_space=pl.ANY)],
        out_specs=vmem,
        scratch_shapes=[
            pltpu.VMEM((modes, points), BF16),
            pltpu.VMEM((rows, window), BF16),
            pltpu.VMEM((2, rows, wide), F32),
            pltpu.VMEM((4, wide), F32),
            pltpu.VMEM((2 * rows, wide), BF16),
            pltpu.VMEM((chunks, rows, CHUNK), F32),
            pltpu.VMEM((chunks, rows, CHUNK), F32),
            pltpu.VMEM((chunks, rows, CHUNK), F32),
            pltpu.VMEM((units, 2 * half, LANES), BF16),
            pltpu.VMEM((n_rad, 2 * half, LANES), BF16),
            pltpu.VMEM((n_rad, 2 * half, LANES), BF16),
            pltpu.VMEM((units, 2 * half, LANES), BF16),
            pltpu.VMEM((2 * rows, padded), BF16),
            dma,
            dma((2,)),
            dma((2,)),
            dma((chunks,)),
            dma((chunks,)),
            dma((units,)),
            dma((n_rad,)),
            dma((n_rad,)),
            dma((units,)),
        ],
        compiler_params=pltpu.CompilerParams(
            collective_id=0, has_side_effects=True, vmem_limit_bytes=48 * 1024 * 1024
        ),
        cost_estimate=pl.CostEstimate(
            flops=8 * rows * points * modes, bytes_accessed=2 * points * modes, transcendentals=0
        ),
    )(occ_rows, cont_rows, degree, radius, radial_weight, harmonics.T)
    return field.reshape(2, radial, points)


def solution(mesh):
    placed = (
        P("orb", None, "rad", None),
        P(None, ("grp", "rad"), None),
        P("orb", None),
        P(),
        P("rad"),
        P("rad"),
        P(),
    )
    return jax.shard_map(
        on_device,
        mesh=mesh,
        in_specs=placed,
        out_specs=P(None, ("grp", "rad"), "orb"),
        check_vma=False,
    )
```

time: 246 us -> 32.9 us (0.13)
  blocking collectives: 92.8 us -> 0 us
  local copies, waits for them, and re-layouts: 66.1 us -> 5.15 us
  matrix products: 40.3 us -> 0 us
  loops' own time: 27.7 us -> 0 us
  Pallas kernels: 0 us -> 25.8 us
  between operations: 14.3 us -> 0.08 us
    all_gather x2 -> x0, blocking collectives: 66.2 us -> none  [carried_in(): pieces = jax.tree.map(lambda part: lax.all_gather(part, axis), value)]
    dot_general x4 -> x0, matrix products: 40.3 us -> none  [the longest x1 15.1 us: radial_potential(): jnp.einsum('kjm,ocjm->ockm', outer_kernel, scaled, precision=lax.Precisio...]
    all_gather x2 -> x0, local copies, waits for them, and re-layouts: 29.4 us -> none  [the longest x1 28.6 us: on_device(): lax.all_gather(harmonics, 'orb', axis=0, tiled=True)]
    another operation x2 -> x0, loops' own time: 27.7 us -> none  [carried_in(): return lax.fori_loop(0, count - 1, step, running)]
    unnamed x2 -> x0, blocking collectives: 26.7 us -> none
    pallas_call x0 -> x1, Pallas kernels: none -> 25.8 us  [on_device(): pl.pallas_call(functools.partial(kernel, n_rad, io, points, modes), out_s...]
    unnamed x26 -> x6, local copies, waits for them, and re-layouts: 19 us -> 3.29 us
    dynamic_slice x21 -> x0, local copies, waits for them, and re-layouts: 8.53 us -> none  [step(): longer = join(running, jax.tree.map(lambda part: part[position], pieces))]
  transfers between devices with their start and end apart: 1 -> 0, of which waited for: 0 -> 0; matrix products, arithmetic and copies ran while one was open for 1% -> 0% of each run, Pallas kernels for 0% -> 0%
where the time goes in v1:
time: 32.9 us; the launch traced here: 32.6 us
  Pallas kernels  25.8 us (78%)
  local copies, waits for them, and re-layouts  5.15 us (16%)
  other arithmetic  1.57 us (5%)
    pallas_call x1, Pallas kernels, on_device(): pl.pallas_call(functools.partial(kernel, n_rad, io, points, modes), out_s...  25.8 us
    unnamed x6, local copies, waits for them, and re-layouts  3.29 us
    transpose x1, local copies, waits for them, and re-layouts, on_device(): jnp.transpose(occupied, (2, 1, 0, 3)).reshape(rows, total_points)  1.09 us
    reduce_sum x1, other arithmetic, degree_of(): return jnp.sum(hits, axis=1)  0.78 us
    transpose x1, other arithmetic, on_device(): jnp.transpose(weighted, (1, 0, 2)).reshape(4, total_points)  0.78 us

profile of v1, /device:TPU:0, one launch (start us, length us, event | category | flops | bytes accessed | tf_op | source)
XLA Modules:
  0.0 32.6 jit_solution(11003536098507336264)
XLA Ops:
  0.0 1.1 %copy.10 = bf16[2,2,16,3470]{3,2,1,0:T(8,128)(2,1)S(1)} copy(bf16[2,2,16,3470]{3,0,1,2:T(2,128)(2,1)} %bitcast.9) | data formatting | bytes 888320 | tf_op jit(solution)/shard_map/transpose | solution.py:300
  1.1 0.8 %multiply_bitcast_fusion = f32[2,2,3470]{2,0,1:T(2,128)S(1)} fusion(bf16[2,2,3470]{2,1,0:T(2,128)(2,1)} %param.8, f32[3470]{0:T(1024)} %param.10), kind=kLoop, calls=%fused_computation.1 | loop fusion | flops 27760 | bytes 97160 | tf_op jit(solution)/shard_map/transpose | solution.py:302
  2.0 0.1 reshape.17
  2.1 0.8 %convert_reduce_fusion = s32[961]{0:T(1024)S(1)} fusion(s32[961]{0:T(1024)} %param.13, s32[30]{0:T(128)S(1)} %add_multiply_fusion), kind=kLoop, calls=%fused_computation | loop fusion | flops 85529 | bytes 7808 | tf_op jit(solution)/shard_map/reduce_sum | solution.py:22
  2.9 0.0 copy-start
  2.9 2.0 %copy-done = bf16[1735,961]{0,1:T(8,128)(2,1)S(1)} copy-done((bf16[1735,961]{0,1:T(8,128)(2,1)S(1)}, bf16[1735,961]{0,1:T(8,128)(2,1)}, u32[]{:S(2)}) %copy-start) | copy-done | bytes 3334694
  4.8 0.0 copy-start.1
  4.8 0.7 %copy-done.1 = f32[2]{0:T(128)S(1)} copy-done((f32[2]{0:T(128)S(1)}, f32[2]{0:T(128)}, u32[]{:S(2)}) %copy-start.1) | copy-done | bytes 32
  5.5 0.0 copy-start.2
  5.5 0.7 %copy-done.2 = f32[2]{0:T(128)S(1)} copy-done((f32[2]{0:T(128)S(1)}, f32[2]{0:T(128)}, u32[]{:S(2)}) %copy-start.2) | copy-done | bytes 32
  6.2 25.8 %shard_map.73 = f32[4,1735]{1,0:T(4,128)S(1)} custom-call(bf16[64,3584]{1,0:T(8,128)(2,1)S(1)} %pad.12.occ_ref, f32[4,3584]{1,0:T(4,128)S(1)} %pad.13.cont_ref, f32[1,1024]{1,0:T(1,128)S(1)} %bitcast.7, f32[2]{0:T(128)S(1)} %copy-done.1, f32[2]{0:T(128)S(1)} %copy-done.2, bf16[961,1735]{1,0:T(8,128)(2,1)S(1)} %bitcast.6), custom_call_target="tpu_custom_call" | custom-call | flops 853675520 | bytes 3334670 | tf_op jit(solution)/shard_map/pallas_call | solution.py:308
  32.0 0.6 %reshape.18 = f32[2,2,1735]{2,1,0:T(2,128)} reshape(f32[4,1735]{1,0:T(4,128)S(1)} %shard_map.73) | data formatting | bytes 55520 | tf_op jit(solution)/shard_map/reshape | solution.py:344
  (6 shorter events, 0.1 us)
Async XLA Ops:
  2.9 2.0 %copy-start = (bf16[1735,961]{0,1:T(8,128)(2,1)S(1)}, bf16[1735,961]{0,1:T(8,128)(2,1)}, u32[]{:S(2)}) copy-start(bf16[1735,961]{0,1:T(8,128)(2,1)} %param.9) | copy-start | bytes 10004014
  4.8 0.7 %copy-start.1 = (f32[2]{0:T(128)S(1)}, f32[2]{0:T(128)}, u32[]{:S(2)}) copy-start(f32[2]{0:T(128)} %radius_ref.1) | copy-start | bytes 28
  5.5 0.7 %copy-start.2 = (f32[2]{0:T(128)S(1)}, f32[2]{0:T(128)}, u32[]{:S(2)}) copy-start(f32[2]{0:T(128)} %weight_ref.1) | copy-start | bytes 28

commit v2 on v1

--- a/solution.py
+++ b/solution.py
@@ -17,15 +17,17 @@
 
 
 def degree_of(harmonic_order):
-    squares = (jnp.arange(1, LMAX + 1) ** 2).astype(jnp.int32)
-    hits = (harmonic_order[:, None] >= squares[None, :]).astype(jnp.int32)
-    return jnp.sum(hits, axis=1)
+    degree = jnp.zeros(harmonic_order.shape, F32)
+    for least in range(1, LMAX + 1):
+        degree += (harmonic_order >= least * least).astype(F32)
+    return degree
 
 
 def kernel(
     n_rad, io, points, modes,
-    occ_ref, cont_ref, degree_ref, radius_ref, weight_ref, table_hbm, out_ref,
-    table, occ_in, occ, cont, dens, m_own, m_send, m_recv, st, inbox, carried, carry, pot,
+    occ_hbm, cont_hbm, angle_hbm, order_hbm, radius_hbm, weight_hbm, table_hbm, out_ref,
+    cont_in, angle, order, padded_order, radius_ref, weight_ref, small_sem,
+    table, occ_raw, occ, cont, dens, m_own, m_send, m_recv, st, inbox, carried, carry, pot,
     table_sem, sib_send, sib_recv, m_send_sem, m_recv_sem, up_send, up_recv, back_send, back_recv,
 ):
     me, core = lax.axis_index("rad"), lax.axis_index("orb")
@@ -35,11 +37,20 @@
     units = st.shape[0]
     stride = n_rad // units
     wide = occ.shape[2]
-    window = occ_in.shape[1]
     base = points // LANES * LANES
     shift = points - base
+    total_points = occ_raw.shape[-1]
     chunks = m_own.shape[0]
 
+    small = [
+        pltpu.make_async_copy(source, target, small_sem.at[place])
+        for place, (source, target) in enumerate((
+            (order_hbm, order), (radius_hbm, radius_ref), (weight_hbm, weight_ref),
+            (cont_hbm, cont_in), (angle_hbm, angle), (occ_hbm, occ_raw.at[0]),
+        ))
+    ]
+    for copy in small:
+        copy.start()
     fetch = pltpu.make_async_copy(table_hbm, table, table_sem)
     fetch.start()
 
@@ -55,8 +66,8 @@
     pl.semaphore_wait(barrier, n_rad)
 
     send_occ = pltpu.make_async_remote_copy(
-        src_ref=occ_ref.at[:, pl.ds(pl.multiple_of(sibling * base, LANES), window)],
-        dst_ref=occ_in,
+        src_ref=occ_hbm,
+        dst_ref=occ_raw.at[1],
         send_sem=sib_send.at[0],
         recv_sem=sib_recv.at[0],
         device_id={"orb": sibling},
@@ -64,7 +75,11 @@
     )
     send_occ.start()
 
-    degree = degree_ref[...]
+    for copy in small:
+        copy.wait()
+    padded_order[...] = jnp.zeros(padded_order.shape, jnp.int32)
+    padded_order[:, :modes] = order[...]
+    degree = degree_of(padded_order[...])
     r0, r1, w0, w1 = radius_ref[0], radius_ref[1], weight_ref[0], weight_ref[1]
     log0 = jnp.log(jnp.full(degree.shape, r0, F32))
     log1 = jnp.log(jnp.full(degree.shape, r1, F32))
@@ -74,10 +89,17 @@
     b0, b1 = jnp.exp(-(degree + 1.0) * log0) * w0, jnp.exp(-(degree + 1.0) * log1) * w1
     factor = FOUR_PI / (2.0 * degree + 1.0)
 
-    mine = pl.ds(pl.multiple_of(core * base, LANES), window)
-
     def align(value):
-        return pltpu.roll(value, lax.rem(window - core * shift, window), 1)[:, :wide]
+        high = jnp.pad(value[:, base:], ((0, 0), (0, base + wide - total_points + LANES)))
+        moved = pltpu.roll(high, high.shape[1] - shift, 1)[:, :wide]
+        return jnp.where(core == 0, value[:, :wide], moved)
+
+    def load_orbitals(slot):
+        for c in range(2):
+            both = occ_raw[slot, :, c].astype(F32)
+            for k in range(2):
+                top = k * half + c * io
+                occ[slot, top : top + io] = align(both[:, k])
 
     def make_density(slot):
         for k in range(2):
@@ -88,14 +110,17 @@
             dens[top : top + io] = (real * c_real + imag * c_imag).astype(BF16)
             dens[top + io : top + half] = (real * c_imag - imag * c_real).astype(BF16)
 
-    cont[...] = align(cont_ref[:, mine])
-    occ[0] = align(occ_ref[:, mine].astype(F32))
+    for c in range(2):
+        wave = align(cont_in[c].astype(F32) * angle[...].reshape(1, total_points))
+        for k in range(2):
+            cont[2 * k + c : 2 * k + c + 1] = wave[k : k + 1]
+    load_orbitals(0)
     make_density(0)
     m_send[chunks - 1] = jnp.zeros(m_send.shape[1:], F32)
     m_own[chunks - 1] = jnp.zeros(m_own.shape[1:], F32)
 
     send_occ.wait()
-    occ[1] = align(occ_in[...].astype(F32))
+    load_orbitals(1)
     make_density(1)
     fetch.wait()
 
@@ -289,30 +314,27 @@
     n_rad = lax.axis_size("rad")
     padded = -(-modes // CHUNK) * CHUNK
     units, chunks = padded // LANES, padded // CHUNK
-    base = points // LANES * LANES
     wide = -(-points // LANES) * LANES
-    window = -(-total_points // LANES) * LANES - base
-    lanes_in = base + window
     rows = 4 * io
     half = 2 * io
 
-    fill = ((0, 0), (0, lanes_in - total_points))
-    occ_rows = jnp.pad(jnp.transpose(occupied, (2, 1, 0, 3)).reshape(rows, total_points), fill)
-    weighted = continuum.astype(F32) * angle_weight
-    cont_rows = jnp.pad(jnp.transpose(weighted, (1, 0, 2)).reshape(4, total_points), fill)
-    degree = jnp.pad(degree_of(harmonic_order).astype(F32), (0, padded - modes))[None]
-
     vmem = pl.BlockSpec(memory_space=pltpu.VMEM)
-    smem = pl.BlockSpec(memory_space=pltpu.SMEM)
     dma = pltpu.SemaphoreType.DMA
     field = pl.pallas_call(
         functools.partial(kernel, n_rad, io, points, modes),
         out_shape=jax.ShapeDtypeStruct((4, points), F32),
-        in_specs=[vmem, vmem, vmem, smem, smem, pl.BlockSpec(memory_space=pl.ANY)],
+        in_specs=[pl.BlockSpec(memory_space=pl.ANY)] * 7,
         out_specs=vmem,
         scratch_shapes=[
+            pltpu.VMEM(continuum.shape, BF16),
+            pltpu.VMEM(angle_weight.shape, F32),
+            pltpu.VMEM((1, modes), jnp.int32),
+            pltpu.VMEM((1, padded), jnp.int32),
+            pltpu.SMEM(radius.shape, F32),
+            pltpu.SMEM(radius.shape, F32),
+            dma((6,)),
             pltpu.VMEM((modes, points), BF16),
-            pltpu.VMEM((rows, window), BF16),
+            pltpu.VMEM((2, *occupied.shape), BF16),
             pltpu.VMEM((2, rows, wide), F32),
             pltpu.VMEM((4, wide), F32),
             pltpu.VMEM((2 * rows, wide), BF16),
@@ -335,12 +357,15 @@
             dma((units,)),
         ],
         compiler_params=pltpu.CompilerParams(
-            collective_id=0, has_side_effects=True, vmem_limit_bytes=48 * 1024 * 1024
+            collective_id=0, has_side_effects=True, vmem_limit_bytes=63 * 1024 * 1024
         ),
         cost_estimate=pl.CostEstimate(
             flops=8 * rows * points * modes, bytes_accessed=2 * points * modes, transcendentals=0
         ),
-    )(occ_rows, cont_rows, degree, radius, radial_weight, harmonics.T)
+    )(
+        occupied, continuum, angle_weight, harmonic_order[None], radius, radial_weight,
+        harmonics.T,
+    )
     return field.reshape(2, radial, points)
 
 

time: 32.9 us -> 27.8 us (0.84)
  local copies, waits for them, and re-layouts: 5.15 us -> 1.38 us
  other arithmetic: 1.57 us -> 0 us
  Pallas kernels: 25.8 us -> 26.3 us
    unnamed x6 -> x0, local copies, waits for them, and re-layouts: 3.29 us -> none
    transpose x2 -> x0, local copies, waits for them, and re-layouts: 1.13 us -> none  [the longest x1 1.09 us: on_device(): jnp.transpose(occupied, (2, 1, 0, 3)).reshape(rows, total_points)]
    reduce_sum x1 -> x0, other arithmetic: 0.78 us -> none  [degree_of(): return jnp.sum(hits, axis=1)]
    transpose x1 -> x0, other arithmetic: 0.78 us -> none  [on_device(): jnp.transpose(weighted, (1, 0, 2)).reshape(4, total_points)]
    reshape x1, local copies, waits for them, and re-layouts: 0.64 us -> 1.38 us  [on_device(): return field.reshape(2, radial, points)]
    pallas_call x1, Pallas kernels: 25.8 us -> 26.3 us  [on_device(): pl.pallas_call(functools.partial(kernel, n_rad, io, points, modes), out_s...]
where the time goes in v2:
time: 27.8 us; the launch traced here: 27.6 us
  Pallas kernels  26.3 us (95%)
  local copies, waits for them, and re-layouts  1.38 us (5%)
    pallas_call x1, Pallas kernels, on_device(): pl.pallas_call(functools.partial(kernel, n_rad, io, points, modes), out_s...  26.3 us
    reshape x1, local copies, waits for them, and re-layouts, on_device(): return field.reshape(2, radial, points)  1.38 us

profile of v2, /device:TPU:0, one launch (start us, length us, event | category | flops | bytes accessed | tf_op | source)
XLA Modules:
  0.0 27.6 jit_solution(2655385892082649616)
XLA Ops:
  0.0 26.3 %shard_map.73 = f32[4,1735]{1,0:T(4,128)} custom-call(bf16[16,2,2,3470]{3,2,1,0:T(2,128)(2,1)} %occ_hbm.1, bf16[2,2,3470]{2,1,0:T(2,128)(2,1)} %cont_hbm.1, f32[3470]{0:T(1024)} %angle_hbm.1, s32[1,961]{1,0:T(1,128)} %bitcast.3, f32[2]{0:T(128)} %radius_hbm.1, f32[2]{0:T(128)} %weight_hbm.1, bf16[961,1735]{1,0:T(8,128)(2,1)} %bitcast.2), custom_call_target="tpu_custom_call" | custom-call | flops 853675520 | bytes 3334670 | tf_op jit(solution)/shard_map/pallas_call | solution.py:323
  26.3 1.4 %reshape.3 = f32[2,2,1735]{2,1,0:T(2,128)} reshape(f32[4,1735]{1,0:T(4,128)} %shard_map.73) | data formatting | bytes 55520 | tf_op jit(solution)/shard_map/reshape | solution.py:369

commit v3 on v2

--- a/solution.py
+++ b/solution.py
@@ -36,6 +36,9 @@
     half = 2 * io
     units = st.shape[0]
     stride = n_rad // units
+    outer_slots = [slot for slot in range(units) if not units // 4 <= slot < 3 * units // 4]
+    inner_slots = [slot for slot in range(units) if units // 4 <= slot < 3 * units // 4]
+    owners = [slot * stride for slot in outer_slots + inner_slots]
     wide = occ.shape[2]
     base = points // LANES * LANES
     shift = points - base
@@ -152,7 +155,7 @@
             dst_ref=inbox.at[me],
             send_sem=up_send.at[u],
             recv_sem=up_recv.at[me],
-            device_id={"rad": u * stride},
+            device_id={"rad": owners[u]},
             device_id_type=MESH,
         )
 
@@ -168,30 +171,22 @@
             st[u, :half] = (a0[:, cols] * m0 + a1[:, cols] * m1).astype(BF16)
             st[u, half:] = (b0[:, cols] * m0 + b1[:, cols] * m1).astype(BF16)
 
-            @pl.when(me != u * stride)
+            @pl.when(me != owners[u])
             def _():
                 up_copy(u).start()
 
-    project(0)
-    for c in range(1, chunks):
-        project(c)
-        summarise(c - 1)
-    summarise(chunks - 1)
-
-    my_unit = me // stride
-
-    def back_copy(r):
+    def back_copy(u, r):
         return pltpu.make_async_remote_copy(
             src_ref=carried.at[r],
-            dst_ref=carry.at[my_unit],
+            dst_ref=carry.at[u],
             send_sem=back_send.at[r],
-            recv_sem=back_recv.at[my_unit],
+            recv_sem=back_recv.at[u],
             device_id={"rad": r},
             device_id_type=MESH,
         )
 
-    def own_unit():
-        inbox[me] = st[my_unit]
+    def own_unit(u):
+        inbox[owners[u]] = st[u]
 
         def receive(r, held):
             @pl.when(r != me)
@@ -216,7 +211,7 @@
 
             @pl.when(r != me)
             def _():
-                back_copy(r).start()
+                back_copy(u, r).start()
 
             return total + inbox[r, half:].astype(F32)
 
@@ -224,22 +219,29 @@
         lax.fori_loop(0, n_rad, receive, 0)
         lax.fori_loop(0, n_rad, rising, zero, unroll=n_rad <= 8)
         lax.fori_loop(0, n_rad, falling, zero, unroll=n_rad <= 8)
-        carry[my_unit] = carried[me]
-
-    if stride == 1:
-        own_unit()
-    else:
-        pl.when(lax.rem(me, stride) == 0)(own_unit)
+        carry[u] = carried[owners[u]]
+
+    def serve(c):
+        for u in range(c * CHUNK // LANES, (c + 1) * CHUNK // LANES):
+            pl.when(me == owners[u])(functools.partial(own_unit, u))
+
+    project(0)
+    for c in range(1, chunks):
+        project(c)
+        summarise(c - 1)
+    summarise(chunks - 1)
+    for c in range(chunks):
+        serve(c)
 
     for u in range(units):
-        @pl.when(me != u * stride)
+        @pl.when(me != owners[u])
         def _():
             pltpu.make_async_remote_copy(
                 src_ref=carried.at[0],
                 dst_ref=carry.at[u],
                 send_sem=back_send.at[0],
                 recv_sem=back_recv.at[u],
-                device_id={"rad": u * stride},
+                device_id={"rad": owners[u]},
                 device_id_type=MESH,
             ).wait_recv()
 
@@ -285,27 +287,24 @@
                 imag = o_real * g_imag + o_imag * g_real
                 real_sum = real if slot == 0 else real_sum + real
                 imag_sum = imag if slot == 0 else imag_sum + imag
-            out_ref[k : k + 1, span] = jnp.sum(real_sum, axis=0, keepdims=True)
-            out_ref[2 + k : 3 + k, span] = jnp.sum(imag_sum, axis=0, keepdims=True)
+            out_ref[0, k : k + 1, span] = jnp.sum(real_sum, axis=0, keepdims=True)
+            out_ref[1, k : k + 1, span] = jnp.sum(imag_sum, axis=0, keepdims=True)
 
     for u in range(units):
-        @pl.when(me != u * stride)
+        @pl.when(me != owners[u])
         def _():
             up_copy(u).wait_send()
 
-    def finish():
-        def sent(r, held):
-            @pl.when(r != me)
-            def _():
-                back_copy(r).wait_send()
-            return held
-
-        lax.fori_loop(0, n_rad, sent, 0)
-
-    if stride == 1:
-        finish()
-    else:
-        pl.when(lax.rem(me, stride) == 0)(finish)
+    for u in range(units):
+        @pl.when(me == owners[u])
+        def _():
+            def sent(r, held):
+                @pl.when(r != me)
+                def _():
+                    back_copy(u, r).wait_send()
+                return held
+
+            lax.fori_loop(0, n_rad, sent, 0)
 
 
 def on_device(occupied, continuum, harmonics, angle_weight, radial_weight, radius, harmonic_order):
@@ -322,7 +321,7 @@
     dma = pltpu.SemaphoreType.DMA
     field = pl.pallas_call(
         functools.partial(kernel, n_rad, io, points, modes),
-        out_shape=jax.ShapeDtypeStruct((4, points), F32),
+        out_shape=jax.ShapeDtypeStruct((2, radial, points), F32),
         in_specs=[pl.BlockSpec(memory_space=pl.ANY)] * 7,
         out_specs=vmem,
         scratch_shapes=[
@@ -366,7 +365,7 @@
         occupied, continuum, angle_weight, harmonic_order[None], radius, radial_weight,
         harmonics.T,
     )
-    return field.reshape(2, radial, points)
+    return field
 
 
 def solution(mesh):

time: 27.8 us -> 24.8 us (0.89)
  Pallas kernels: 26.3 us -> 23.3 us
    pallas_call x1, Pallas kernels: 26.3 us -> 23.3 us  [on_device(): pl.pallas_call(functools.partial(kernel, n_rad, io, points, modes), out_s...]
    reshape x1 -> x0, local copies, waits for them, and re-layouts: 1.38 us -> none  [on_device(): return field.reshape(2, radial, points)]
    unnamed x0 -> x1, local copies, waits for them, and re-layouts: none -> 1.36 us
where the time goes in v3:
time: 24.8 us; the launch traced here: 24.6 us
  Pallas kernels  23.3 us (94%)
  local copies, waits for them, and re-layouts  1.36 us (5%)
    pallas_call x1, Pallas kernels, on_device(): pl.pallas_call(functools.partial(kernel, n_rad, io, points, modes), out_s...  23.3 us
    unnamed x1, local copies, waits for them, and re-layouts  1.36 us

profile of v3, /device:TPU:0, one launch (start us, length us, event | category | flops | bytes accessed | tf_op | source)
XLA Modules:
  0.0 24.6 jit_solution(16754906120087099438)
XLA Ops:
  0.0 23.3 %shard_map.73 = f32[2,2,1735]{2,1,0:T(2,128)} custom-call(bf16[16,2,2,3470]{3,2,1,0:T(2,128)(2,1)} %occ_hbm.1, bf16[2,2,3470]{2,1,0:T(2,128)(2,1)} %cont_hbm.1, f32[3470]{0:T(1024)} %angle_hbm.1, s32[1,961]{1,0:T(1,128)} %bitcast.3, f32[2]{0:T(128)} %radius_hbm.1, f32[2]{0:T(128)} %weight_hbm.1, bf16[961,1735]{1,0:T(8,128)(2,1)} %bitcast.2), custom_call_target="tpu_custom_call" | custom-call | flops 853675520 | bytes 3334670 | tf_op jit(solution)/shard_map/pallas_call | solution.py:322
  23.3 1.4 %copy.9 = f32[2,2,1735]{2,1,0:T(2,128)} copy(f32[2,2,1735]{2,1,0:T(2,128)} %shard_map.73) | data formatting | bytes 55520

commit v4 on v3

--- a/solution.py
+++ b/solution.py
@@ -36,9 +36,9 @@
     half = 2 * io
     units = st.shape[0]
     stride = n_rad // units
-    outer_slots = [slot for slot in range(units) if not units // 4 <= slot < 3 * units // 4]
-    inner_slots = [slot for slot in range(units) if units // 4 <= slot < 3 * units // 4]
-    owners = [slot * stride for slot in outer_slots + inner_slots]
+    owners = []
+    for slot in range(units // 2):
+        owners += [slot * stride, (units - 1 - slot) * stride]
     wide = occ.shape[2]
     base = points // LANES * LANES
     shift = points - base

time: 24.8 us -> 24.2 us (0.976)
  Pallas kernels: 23.3 us -> 22.6 us
    pallas_call x1, Pallas kernels: 23.3 us -> 22.6 us  [on_device(): pl.pallas_call(functools.partial(kernel, n_rad, io, points, modes), out_s...]
where the time goes in v4:
time: 24.2 us; the launch traced here: 24 us
  Pallas kernels  22.6 us (93%)
  local copies, waits for them, and re-layouts  1.36 us (6%)
    pallas_call x1, Pallas kernels, on_device(): pl.pallas_call(functools.partial(kernel, n_rad, io, points, modes), out_s...  22.6 us
    unnamed x1, local copies, waits for them, and re-layouts  1.36 us

profile of v4, /device:TPU:0, one launch (start us, length us, event | category | flops | bytes accessed | tf_op | source)
XLA Modules:
  0.0 24.0 jit_solution(6839603823947810055)
XLA Ops:
  0.0 22.6 %shard_map.73 = f32[2,2,1735]{2,1,0:T(2,128)} custom-call(bf16[16,2,2,3470]{3,2,1,0:T(2,128)(2,1)} %occ_hbm.1, bf16[2,2,3470]{2,1,0:T(2,128)(2,1)} %cont_hbm.1, f32[3470]{0:T(1024)} %angle_hbm.1, s32[1,961]{1,0:T(1,128)} %bitcast.3, f32[2]{0:T(128)} %radius_hbm.1, f32[2]{0:T(128)} %weight_hbm.1, bf16[961,1735]{1,0:T(8,128)(2,1)} %bitcast.2), custom_call_target="tpu_custom_call" | custom-call | flops 853675520 | bytes 3334670 | tf_op jit(solution)/shard_map/pallas_call | solution.py:322
  22.6 1.4 %copy.9 = f32[2,2,1735]{2,1,0:T(2,128)} copy(f32[2,2,1735]{2,1,0:T(2,128)} %shard_map.73) | data formatting | bytes 55520

commit v5 on v4

--- a/solution.py
+++ b/solution.py
@@ -11,7 +11,7 @@
 FOUR_PI = 12.566370614359172
 MESH = pl.DeviceIdType.MESH
 LANES = 128
-CHUNK = 256
+CHUNK = 512
 F32 = jnp.float32
 BF16 = jnp.bfloat16
 
@@ -202,6 +202,7 @@
             return held
 
         def rising(r, total):
+            receive(r, 0)
             carried[r, :half] = total.astype(BF16)
             return total + inbox[r, :half].astype(F32)
 
@@ -216,7 +217,6 @@
             return total + inbox[r, half:].astype(F32)
 
         zero = jnp.zeros((half, LANES), F32)
-        lax.fori_loop(0, n_rad, receive, 0)
         lax.fori_loop(0, n_rad, rising, zero, unroll=n_rad <= 8)
         lax.fori_loop(0, n_rad, falling, zero, unroll=n_rad <= 8)
         carry[u] = carried[owners[u]]

time: 24.2 us -> 24.1 us (level)
  no operation moved by 1% of the time
where the time goes in v5:
time: 24.1 us; the launch traced here: 23.9 us
  Pallas kernels  22.6 us (94%)
  local copies, waits for them, and re-layouts  1.36 us (6%)
    pallas_call x1, Pallas kernels, on_device(): pl.pallas_call(functools.partial(kernel, n_rad, io, points, modes), out_s...  22.6 us
    unnamed x1, local copies, waits for them, and re-layouts  1.36 us

profile of v5, /device:TPU:0, one launch (start us, length us, event | category | flops | bytes accessed | tf_op | source)
XLA Modules:
  0.0 23.9 jit_solution(4770724631824907905)
XLA Ops:
  0.0 22.6 %shard_map.73 = f32[2,2,1735]{2,1,0:T(2,128)} custom-call(bf16[16,2,2,3470]{3,2,1,0:T(2,128)(2,1)} %occ_hbm.1, bf16[2,2,3470]{2,1,0:T(2,128)(2,1)} %cont_hbm.1, f32[3470]{0:T(1024)} %angle_hbm.1, s32[1,961]{1,0:T(1,128)} %bitcast.3, f32[2]{0:T(128)} %radius_hbm.1, f32[2]{0:T(128)} %weight_hbm.1, bf16[961,1735]{1,0:T(8,128)(2,1)} %bitcast.2), custom_call_target="tpu_custom_call" | custom-call | flops 853675520 | bytes 3334670 | tf_op jit(solution)/shard_map/pallas_call | solution.py:322
  22.6 1.4 %copy.9 = f32[2,2,1735]{2,1,0:T(2,128)} copy(f32[2,2,1735]{2,1,0:T(2,128)} %shard_map.73) | data formatting | bytes 55520
